TPU v7x, 32 devices: a whole 2x2x4 slice. The times are simulated.
32 devices in a mesh: req: 8 (over z, x), mlp: 4 (over y, core).
Axes of the slice: x: 2, y: 2, z: 4, core: 2. Of those that a mesh axis runs over, the one named last changes fastest.
Arguments:
- tokens: bfloat16 [4096, 4096], P('req'), may hold values from -16 to 16
- grid_sides: int32 [16, 2], P('req'), may hold values from 10 to 14, as said below
- offsets: int32 [16], P('req'), may hold values from 0 to 201, as said below
- merge_rows: int32 [1024, 4], P('req'), may hold values from 0 to 401, as said below
- routes: int32 [1024, 1], replicated, may hold values from 0 to 7; in each aligned block of 128 rows (0 to 127, 128 to 255, ...) at most 16 rows name the same one
- norm_gain: float32 [2, 4096], replicated, may hold values from 0.5 to 1.5
- norm_bias: float32 [2, 4096], replicated, may hold values from -1.5 to 1.5
- layer_scale: float32 [2, 4096], replicated, may hold values from 0.2 to 1
- qkv_weight: bfloat16 [4096, 6144], P('req', 'mlp'), may hold values from -2.34375 to 2.34375
- out_weight: bfloat16 [2048, 4096], P('mlp', 'req'), may hold values from -0.125 to 0.125
- gate_up: bfloat16 [2, 4096, 4096], P(None, 'req', 'mlp'), may hold values from -0.09375 to 0.09375
- down_weight: bfloat16 [4096, 4096], P('mlp', 'req'), may hold values from -0.09375 to 0.09375
- merge_gain: float32 [4, 4096], P(None, 'mlp'), may hold values from 0.5 to 1.5
- merge_bias: float32 [4, 4096], P(None, 'mlp'), may hold values from -1.5 to 1.5
- merge_weight: bfloat16 [4, 4096, 2048], P(None, 'mlp', 'req'), may hold values from -0.1875 to 0.1875
Outputs:
- embeds: bfloat16 [1024, 2048], P('req', 'mlp')
- token_norms: float32 [1024], P('req')
- max_logits: float32 [16, 16], P('req', 'mlp')
Inputs may be any that keep to these rules, and one draw needn't show every extreme that they name: `grid_sides`: sides are even; the first 2 of all 16 images are 14 x 14 and the last image is 10 x 10. `offsets`: the images of a group are packed in order from in-group row 0: image g * 2 + j starts at the sum of 5 + h w over images g * 2 to g * 2 + j - 1. `merge_rows`: for slot k of group g, image i = g * 2 + k div 64 of grid h x w at offset o and m = k mod 64: if m < (h / 2)(w / 2), the entries are o + 5 + (2 a + e) w + 2 b + f for (e, f) = (0, 0), (0, 1), (1, 0), (1, 1), with a = m div (w / 2), b = m mod (w / 2); otherwise all four are 0. `routes`: among the 128 slots of one group, no value appears more than 16 times.
All inputs are finite; a program needn't handle non-finite values.
Results may differ from a plain program's by a relative error of at most 0.017.
Values may be sent and summed in bfloat16 or wider, within the bound.
A program may use at most 128 MiB of HBM per device.

v0:
```python
import math
import jax
import jax.numpy as jnp
from jax import lax
from jax.sharding import PartitionSpec as P

HEAD = 128
OUT = 2048
MSLOT = 64
CAP = 16
EPS = 1e-06


def layer_norm(values, scale_vec, shift_vec):
    center = jnp.mean(values, axis=-1, keepdims=True)
    offset_vals = values - center
    spread = jnp.mean(offset_vals * offset_vals, axis=-1, keepdims=True)
    return offset_vals * lax.rsqrt(spread + EPS) * scale_vec + shift_vec


def row_layout(grid_part, starts, row_count, head_size):
    position = jnp.arange(row_count, dtype=jnp.int32)
    lengths = 5 + grid_part[:, 0] * grid_part[:, 1]
    inside = (
        (position[:, None] >= starts[None, :]) & (position[:, None] < (starts + lengths)[None, :])
    ).astype(jnp.int32)
    present = jnp.sum(inside, axis=1)
    numbers = jnp.arange(grid_part.shape[0], dtype=jnp.int32)
    image_id = jnp.sum(inside * numbers[None, :], axis=1) + present - 1
    local_row = position - jnp.sum(inside * starts[None, :], axis=1)
    height = jnp.sum(inside * grid_part[None, :, 0], axis=1) + 1 - present
    breadth = jnp.sum(inside * grid_part[None, :, 1], axis=1) + 1 - present
    is_patch = (local_row >= 5) & (present > 0)
    patch_idx = jnp.maximum(local_row - 5, 0)
    coord_y = jnp.where(
        is_patch,
        (2.0 * (patch_idx // breadth).astype(jnp.float32) + 1.0) / height.astype(jnp.float32) - 1.0,
        0.0,
    )
    coord_x = jnp.where(
        is_patch,
        (2.0 * (patch_idx % breadth).astype(jnp.float32) + 1.0) / breadth.astype(jnp.float32) - 1.0,
        0.0,
    )
    quarter = head_size // 4
    frequency = math.pi * 100.0 ** (-jnp.arange(quarter, dtype=jnp.float32) / quarter)
    angle_y = (coord_y[:, None] * frequency[None, :])[:, None, :]
    angle_x = (coord_x[:, None] * frequency[None, :])[:, None, :]
    return (image_id, (jnp.cos(angle_y), jnp.sin(angle_y), jnp.cos(angle_x), jnp.sin(angle_x)))


def rotate(vectors, tables):
    cos_y, sin_y, cos_x, sin_x = tables
    quarter = vectors.shape[-1] // 4
    upper_y = vectors[..., :quarter]
    lower_y = vectors[..., quarter : 2 * quarter]
    upper_x = vectors[..., 2 * quarter : 3 * quarter]
    lower_x = vectors[..., 3 * quarter :]
    return jnp.concatenate(
        [
            upper_y * cos_y - lower_y * sin_y,
            upper_y * sin_y + lower_y * cos_y,
            upper_x * cos_x - lower_x * sin_x,
            upper_x * sin_x + lower_x * cos_x,
        ],
        axis=-1,
    )


def attend(queries, key_rows, values, image_id, numbers):
    scores = jnp.einsum(
        "qhd,khd->hqk", queries, key_rows, preferred_element_type=jnp.float32
    ) / math.sqrt(queries.shape[-1])
    same_image = image_id[:, None] == image_id[None, :]
    scores = jnp.where(same_image[None], scores, -jnp.inf)
    row_peak = jnp.max(scores, axis=-1)
    expo_vals = jnp.exp(scores - row_peak[..., None])
    weights = (expo_vals / jnp.sum(expo_vals, axis=-1, keepdims=True)).astype(jnp.bfloat16)
    attended = jnp.einsum(
        "hqk,khd->qhd", weights, values, preferred_element_type=jnp.float32
    ).astype(jnp.bfloat16)
    owned = image_id[None, None, :] == numbers[:, None, None]
    logits = jnp.max(jnp.where(owned, row_peak[None], -jnp.inf), axis=-1)
    return (attended, logits)


def on_device(
    tokens,
    grid_sides,
    offsets,
    merge_rows,
    routes,
    norm_gain,
    norm_bias,
    layer_scale,
    qkv_weight,
    out_weight,
    gate_up,
    down_weight,
    merge_gain,
    merge_bias,
    merge_weight,
):
    row_count = tokens.shape[0]
    model_width = tokens.shape[1]
    groups = lax.axis_size("req")
    shards = lax.axis_size("mlp")
    group_id = lax.axis_index("req")
    member = lax.axis_index("mlp")
    piece_width = model_width // shards
    start_col = member * piece_width
    slot_count = merge_rows.shape[0]
    numbers = jnp.arange(grid_sides.shape[0], dtype=jnp.int32)
    image_id, tables = row_layout(grid_sides, offsets, row_count, HEAD)
    normed = layer_norm(tokens.astype(jnp.float32), norm_gain[0], norm_bias[0]).astype(jnp.bfloat16)
    columns = normed
    mixed_qkv = jnp.dot(
        columns,
        lax.all_gather(qkv_weight, "req", axis=0, tiled=True),
        preferred_element_type=jnp.float32,
    )
    heads_here = qkv_weight.shape[1] // (3 * HEAD)
    mixed_qkv = mixed_qkv.reshape(row_count, heads_here, 3, HEAD)
    queries = rotate(mixed_qkv[:, :, 0], tables).astype(jnp.bfloat16)
    key_rows = rotate(mixed_qkv[:, :, 1], tables).astype(jnp.bfloat16)
    values = mixed_qkv[:, :, 2].astype(jnp.bfloat16)
    attended, logits = attend(queries, key_rows, values, image_id, numbers)
    attended_flat = attended.reshape(row_count, heads_here * HEAD)
    head_terms = jnp.dot(
        attended_flat,
        lax.all_gather(out_weight, "req", axis=1, tiled=True),
        preferred_element_type=jnp.float32,
    )
    attn_sum = lax.psum(head_terms.astype(jnp.bfloat16), "mlp").astype(jnp.float32)
    residual = (tokens.astype(jnp.float32) + layer_scale[0] * attn_sum).astype(jnp.bfloat16)
    resid_piece = lax.dynamic_slice_in_dim(residual, start_col, piece_width, 1)
    normed_two = layer_norm(residual.astype(jnp.float32), norm_gain[1], norm_bias[1]).astype(
        jnp.bfloat16
    )
    columns = normed_two
    gate_pair = jnp.einsum(
        "rk,pkn->prn",
        columns,
        lax.all_gather(gate_up, "req", axis=1, tiled=True),
        preferred_element_type=jnp.float32,
    )
    hidden = (jax.nn.silu(gate_pair[0]) * gate_pair[1]).astype(jnp.bfloat16)
    hidden_terms = jnp.dot(
        hidden,
        lax.all_gather(down_weight, "req", axis=1, tiled=True),
        preferred_element_type=jnp.float32,
    )
    ffn_piece = lax.psum_scatter(
        hidden_terms.astype(jnp.bfloat16), "mlp", scatter_dimension=1, tiled=True
    ).astype(jnp.float32)
    own_scale_two = lax.dynamic_slice_in_dim(layer_scale[1], start_col, piece_width, 0)
    final_piece = (resid_piece.astype(jnp.float32) + own_scale_two * ffn_piece).astype(jnp.bfloat16)
    merged = final_piece[merge_rows].astype(jnp.float32)
    totals, squares = lax.psum(
        (jnp.sum(merged, axis=(1, 2)), jnp.sum(merged * merged, axis=(1, 2))), "mlp"
    )
    center = totals / (4 * model_width)
    spread = squares / (4 * model_width) - center * center
    scaled = (
        (merged - center[:, None, None]) * lax.rsqrt(spread + EPS)[:, None, None] * merge_gain[None]
        + merge_bias[None]
    ).astype(jnp.bfloat16)
    scaled_flat = scaled.reshape(slot_count, 4 * piece_width)
    piece_rows = lax.all_gather(merge_weight, "req", axis=2, tiled=True)
    merge_terms = jnp.dot(
        scaled_flat,
        piece_rows.reshape(4 * piece_width, piece_rows.shape[2]),
        preferred_element_type=jnp.float32,
    )
    projected = lax.psum_scatter(
        merge_terms.astype(jnp.bfloat16), "mlp", scatter_dimension=1, tiled=True
    ).astype(jnp.float32)
    slot_ids = jnp.arange(slot_count, dtype=jnp.int32)
    owner_grid = grid_sides[slot_ids // MSLOT]
    is_live = slot_ids % MSLOT < owner_grid[:, 0] // 2 * (owner_grid[:, 1] // 2)
    projected = jnp.where(is_live[:, None], projected, 0.0).astype(jnp.bfloat16)
    out_cols = projected.shape[1]
    own_routes = lax.dynamic_slice_in_dim(routes, group_id * slot_count, slot_count, 0)[:, 0]
    onehot = (own_routes[:, None] == jnp.arange(groups, dtype=jnp.int32)[None, :]).astype(jnp.int32)
    before = jnp.cumsum(onehot, axis=0) - onehot
    ranks = jnp.sum(before * onehot, axis=1)
    send_rows = (
        jnp.zeros((groups * CAP, out_cols), jnp.bfloat16)
        .at[own_routes * CAP + ranks]
        .set(projected)
    )
    received = lax.all_to_all(
        send_rows.reshape(groups, CAP, out_cols), "req", split_axis=0, concat_axis=0, tiled=True
    )
    embeds = received.reshape(groups * CAP, out_cols)
    row_squares = jnp.sum(jnp.square(embeds.astype(jnp.float32)), axis=1)
    total_squares = lax.psum(row_squares, "mlp")
    token_norms = jnp.sqrt(total_squares / OUT + EPS)
    return (embeds, token_norms, logits)


def solution(mesh):
    placed = (
        P("req", None),
        P("req", None),
        P("req"),
        P("req", None),
        P(),
        P(),
        P(),
        P(),
        P("req", "mlp"),
        P("mlp", "req"),
        P(None, "req", "mlp"),
        P("mlp", "req"),
        P(None, "mlp"),
        P(None, "mlp"),
        P(None, "mlp", "req"),
    )
    return jax.shard_map(
        on_device,
        mesh=mesh,
        in_specs=placed,
        out_specs=(P("req", "mlp"), P("req"), P("req", "mlp")),
        check_vma=False,
    )
```

profile of v0, /device:TPU:0, one launch (start us, length us, event | category | flops | bytes accessed | tf_op | source)
XLA Modules:
  0.0 1053.9 jit_solution(7051907031724275753)
XLA Ops:
  8.7 1.1 slice_reduce_fusion
  11.5 2.8 convert_reduce_fusion
  14.3 1.2 fusion.4
  15.9 3.0 multiply_cosine_fusion.1
  19.0 170.4 %all-gather.6.cloned.1.call-done = bf16[4096,1536]{1,0:T(8,128)(2,1)} async-done(((bf16[512,1536]{1,0:T(8,128)(2,1)}), bf16[4096,1536]{1,0:T(8,128)(2,1)}) %all-gather.6.cloned.1.call-update) | async-done | bytes 12582928 | tf_op jit(solution)/shard_map/all_gather | solution.py:119
  189.4 11.7 %fusion.16 = f32[512,1536]{0,1:T(8,128)S(1)} fusion(bf16[4096,1536]{1,0:T(8,128)(2,1)} %all-gather.6.cloned.1.call-done, bf16[512,4096]{1,0:T(8,128)(2,1)} %param.15, f32[4096]{0:T(1024)S(1)} %bitcast.60, f32[4096]{0:T(1024)S(1)} %bitcast.59, f32[512]{0:T(512)S(1)} %add_rsqrt_fusion.1, f32[512]{0:T(512)S(1)} %broadcast_multiply_fusion.1), kind=kOutput, calls=%fused_computation.25 | convolution fusion | flops 6455033856 | bytes 19959808 | tf_op jit(solution)/shard_map/dot_general | solution.py:117
  201.2 1.5 copy-done.8
  203.4 2.2 subtract_convert_fusion.3
  206.5 2.1 fusion.26
  209.5 2.7 fusion.39
  212.2 52.4 %all-gather.8.cloned.1.call-done = bf16[512,4096]{1,0:T(8,128)(2,1)} async-done(((bf16[512,512]{1,0:T(8,128)(2,1)}), bf16[512,4096]{1,0:T(8,128)(2,1)}) %all-gather.8.cloned.1.call-update) | async-done | bytes 4194320 | tf_op jit(solution)/shard_map/all_gather | solution.py:131
  264.6 6.5 convolution_convert_fusion.1
  272.7 82.3 %all-reduce.3.cloned.1.call-done = bf16[512,4096]{1,0:T(8,128)(2,1)} async-done(((bf16[512,4096]{1,0:T(8,128)(2,1)}), bf16[512,4096]{1,0:T(8,128)(2,1)}) %all-reduce.3.cloned.1.call-update) | async-done | bytes 4194320 | tf_op jit(solution)/shard_map/psum | solution.py:134
  355.0 5.6 convert_reduce_fusion.1
  360.6 1.9 copy-done.3
  362.5 1.2 fusion.8
  363.7 221.3 %all-gather.10.cloned.1.call-done = bf16[2,4096,1024]{2,1,0:T(8,128)(2,1)} async-done(((bf16[2,512,1024]{2,1,0:T(8,128)(2,1)}), bf16[2,4096,1024]{2,1,0:T(8,128)(2,1)}) %all-gather.10.cloned.1.call-update) | async-done | bytes 16777232 | tf_op jit(solution)/shard_map/all_gather | solution.py:144
  585.1 15.0 %fusion.29 = f32[2,512,1024]{2,1,0:T(8,128)} fusion(bf16[2,4096,1024]{2,1,0:T(8,128)(2,1)} %all-gather.10.cloned.1.call-done, bf16[512,4096]{1,0:T(8,128)(2,1)} %copy-done.3, f32[4096]{0:T(1024)S(1)} %bitcast.58, f32[4096]{0:T(1024)S(1)} %bitcast.57, f32[512]{0:T(512)S(1)} %add_rsqrt_fusion, f32[512]{0:T(512)S(1)} %broadcast_multiply_fusion), kind=kOutput, calls=%fused_computation.41 | convolution fusion | flops 8602517504 | bytes 25202688 | tf_op jit(solution)/shard_map/rk,pkn->prn/dot_general | solution.py:141
  600.1 110.7 %all-gather.12.cloned.1.call-done = bf16[1024,4096]{1,0:T(8,128)(2,1)} async-done(((bf16[1024,512]{1,0:T(8,128)(2,1)}), bf16[1024,4096]{1,0:T(8,128)(2,1)}) %all-gather.12.cloned.1.call-update) | async-done | bytes 8388624 | tf_op jit(solution)/shard_map/all_gather | solution.py:150
  710.8 11.2 %convolution_convert_fusion = bf16[512,4096]{1,0:T(8,128)(2,1)} fusion(bf16[1024,4096]{1,0:T(8,128)(2,1)} %all-gather.12.cloned.1.call-done, f32[2,512,1024]{2,1,0:T(8,128)} %fusion.29), kind=kOutput, calls=%fused_computation.21 | convolution fusion | flops 4300210176 | bytes 16777216 | tf_op jit(solution)/shard_map/dot_general | solution.py:148
  723.3 41.5 %reduce-scatter.3.cloned.1.call-done = bf16[512,1024]{1,0:T(8,128)(2,1)} async-done(((bf16[512,4096]{1,0:T(8,128)(2,1)}), bf16[512,1024]{1,0:T(8,128)(2,1)}) %reduce-scatter.3.cloned.1.call-update) | async-done | bytes 1048592 | tf_op jit(solution)/shard_map/reduce_scatter | solution.py:153
  764.8 2.0 add_convert_fusion
  766.8 2.1 gather_fusion.1
  770.0 1.0 multiply_reduce_fusion
  771.0 5.7 all-reduce
  776.8 217.8 %all-gather.14.cloned.1.call-done = bf16[4,1024,2048]{2,1,0:T(8,128)(2,1)} async-done(((bf16[4,1024,256]{2,1,0:T(8,128)(2,1)}), bf16[4,1024,2048]{2,1,0:T(8,128)(2,1)}) %all-gather.14.cloned.1.call-update) | async-done | bytes 16777232 | tf_op jit(solution)/shard_map/all_gather | solution.py:169
  994.6 10.1 fusion.28
  1006.6 18.2 %reduce-scatter.5.cloned.1.call-done = bf16[128,512]{1,0:T(8,128)(2,1)} async-done(((bf16[128,2048]{1,0:T(8,128)(2,1)}), bf16[128,512]{1,0:T(8,128)(2,1)}) %reduce-scatter.5.cloned.1.call-update) | async-done | bytes 131088 | tf_op jit(solution)/shard_map/reduce_scatter | solution.py:175
  1024.8 2.1 scatter_custom_fusion
  1026.9 5.5 all-to-all-start
  1033.1 6.7 all-to-all-done
  1040.0 5.9 psum.31
  (90 shorter events, 14.0 us)
Async XLA Ops:
  7.2 997.6 %copy-start = (s32[1024,1]{0,1:T(1,128)S(1)}, s32[1024,1]{0,1:T(1,128)}, u32[]{:S(2)}) copy-start(s32[1024,1]{0,1:T(1,128)} %param.19) | copy-start | bytes 12292
  7.2 182.2 %all-gather.6.cloned.1.call-start = ((), (), s32[]{:S(2)}) async-start(), calls=%async_computation.3 | async-start | bytes 14155776 | tf_op jit(solution)/shard_map/all_gather | solution.py:119
  7.9 256.7 %all-gather.8.cloned.1.call-start = ((), (), s32[]{:S(2)}) async-start(), calls=%async_computation.4 | async-start | bytes 4718592 | tf_op jit(solution)/shard_map/all_gather | solution.py:131
  8.7 346.4 %all-reduce.3.cloned.1.call-start = ((), (), s32[]{:S(2)}) async-start(), calls=%async_computation.5 | async-start | bytes 8388608 | tf_op jit(solution)/shard_map/psum | solution.py:134
  8.7 5.6 copy-start.2
  11.4 7.5 copy-start.11
  11.4 7.5 copy-start.12
  201.0 1.7 copy-start.8
  203.4 2.2 copy-start.4
  203.4 2.2 copy-start.5
  203.4 2.2 copy-start.6
  203.4 2.2 copy-start.7
  271.2 1.5 copy-start.13
  271.2 313.9 %all-gather.10.cloned.1.call-start = ((), (), s32[]{:S(2)}) async-start(), calls=%async_computation.6 | async-start | bytes 18874368 | tf_op jit(solution)/shard_map/all_gather | solution.py:144
  271.8 439.0 %all-gather.12.cloned.1.call-start = ((), (), s32[]{:S(2)}) async-start(), calls=%async_computation.7 | async-start | bytes 9437184 | tf_op jit(solution)/shard_map/all_gather | solution.py:150
  272.4 492.4 %reduce-scatter.3.cloned.1.call-start = ((), (), s32[]{:S(2)}) async-start(), calls=%async_computation.8 | async-start | bytes 5242880 | tf_op jit(solution)/shard_map/reduce_scatter | solution.py:153
  360.6 1.9 copy-start.3
  721.9 1.1 copy-start.14
  721.9 272.7 %all-gather.14.cloned.1.call-start = ((), (), s32[]{:S(2)}) async-start(), calls=%async_computation.9 | async-start | bytes 18874368 | tf_op jit(solution)/shard_map/all_gather | solution.py:169
  722.7 302.1 %reduce-scatter.5.cloned.1.call-start = ((), (), s32[]{:S(2)}) async-start(), calls=%async_computation.10 | async-start | bytes 655360 | tf_op jit(solution)/shard_map/reduce_scatter | solution.py:175
  768.8 225.8 %copy-start.9 = (f32[4,1024]{1,0:T(4,128)S(1)}, f32[4,1024]{1,0:T(4,128)}, u32[]{:S(2)}) copy-start(f32[4,1024]{1,0:T(4,128)} %param.28) | copy-start | bytes 49156
  768.8 225.8 %copy-start.10 = (f32[4,1024]{1,0:T(4,128)S(1)}, f32[4,1024]{1,0:T(4,128)}, u32[]{:S(2)}) copy-start(f32[4,1024]{1,0:T(4,128)} %param.27) | copy-start | bytes 49156
  994.6 11.0 %copy-start.1 = (s32[2,2]{1,0:T(2,128)S(1)}, s32[2,2]{1,0:T(2,128)}, u32[]{:S(2)}) copy-start(s32[2,2]{1,0:T(2,128)} %param.16) | copy-start | bytes 52
  1026.9 12.9 %all-to-all-start = ((bf16[8,16,512]{2,1,0:T(8,128)(2,1)}), bf16[8,16,512]{2,1,0:T(8,128)(2,1)S(1)}, u32[]{:S(2)}, u32[]{:S(2)}) async-start(bf16[8,16,512]{2,1,0:T(8,128)(2,1)} %bitcast.18), calls=%async_computation.2 | async-start | bytes 262144 | tf_op jit(solution)/shard_map/all_to_all | solution.py:192
Sparse Core Ops, SparseCore 0:
  10.2 179.1 all-gather.5
  191.4 73.1 all-gather.7
  271.3 83.6 all-reduce.2
  357.3 227.7 all-gather.9
  587.1 123.5 all-gather.11
  722.1 42.6 reduce-scatter.2
  766.8 227.7 all-gather.13
  1004.9 19.8 reduce-scatter.4
where the time goes:
time: 1050 us
  waiting for transfers between devices  925 us (88%)
  matrix products  59.2 us (6%)
  other arithmetic  27.4 us (3%)
  between operations  14.5 us (1%)
  blocking collectives  11.6 us (1%)
    all_gather x1, waiting for transfers between devices, on_device(): lax.all_gather(gate_up, 'req', axis=1, tiled=True)  221 us
    all_gather x1, waiting for transfers between devices, on_device(): piece_rows = lax.all_gather(merge_weight, 'req', axis=2, tiled=True)  218 us
    all_gather x1, waiting for transfers between devices, on_device(): lax.all_gather(qkv_weight, 'req', axis=0, tiled=True)  170 us
    all_gather x1, waiting for transfers between devices, on_device(): lax.all_gather(down_weight, 'req', axis=1, tiled=True)  111 us
    psum x1, waiting for transfers between devices, on_device(): lax.psum(head_terms.astype(jnp.bfloat16), 'mlp').astype(jnp.float32)  82.3 us
    all_gather x1, waiting for transfers between devices, on_device(): lax.all_gather(out_weight, 'req', axis=1, tiled=True)  52.4 us
    reduce_scatter x1, waiting for transfers between devices, on_device(): lax.psum_scatter(hidden_terms.astype(jnp.bfloat16), 'mlp', scatter_dimens...  41.5 us
  transfers between devices with their start and end apart: 9, of which 9 were waited for; matrix products, arithmetic and copies ran while one was open for 6% of the time, Pallas kernels for 0%

commit v1 on v0

--- a/solution.py
+++ b/solution.py
@@ -166,7 +166,12 @@
         + merge_bias[None]
     ).astype(jnp.bfloat16)
     scaled_flat = scaled.reshape(slot_count, 4 * piece_width)
-    piece_rows = lax.all_gather(merge_weight, "req", axis=2, tiled=True)
+    ring = [merge_weight]
+    for hop in range(7):
+        ring.append(lax.ppermute(ring[-1], "req", [(dev, (dev + 1) % 8) for dev in range(8)]))
+    piece_rows = jnp.roll(
+        jnp.concatenate(ring[::-1], axis=2), (lax.axis_index("req") + 1) * ring[0].shape[2], axis=2
+    )
     merge_terms = jnp.dot(
         scaled_flat,
         piece_rows.reshape(4 * piece_width, piece_rows.shape[2]),

time: 1050 us -> 1060 us (level)
  waiting for transfers between devices: 925 us -> 883 us
  local copies, waits for them, and re-layouts: 10.2 us -> 51.5 us
    ppermute x0 -> x7, waiting for transfers between devices: none -> 375 us  [on_device(): lax.ppermute(ring[-1], 'req', [(dev, (dev + 1) % 8) for dev in range(8)])]
    all_gather x1 -> x0, waiting for transfers between devices: 218 us -> none  [on_device(): piece_rows = lax.all_gather(merge_weight, 'req', axis=2, tiled=True)]
    psum x1, waiting for transfers between devices: 82.3 us -> 0.02 us  [on_device(): lax.psum(head_terms.astype(jnp.bfloat16), 'mlp').astype(jnp.float32)]
    all_gather x1, waiting for transfers between devices: 221 us -> 146 us  [on_device(): lax.all_gather(gate_up, 'req', axis=1, tiled=True)]
    reduce_scatter x1, waiting for transfers between devices: 41.5 us -> 0.01 us  [on_device(): lax.psum_scatter(hidden_terms.astype(jnp.bfloat16), 'mlp', scatter_dimens...]
    unnamed x34 -> x63, local copies, waits for them, and re-layouts: 4.89 us -> 44.6 us
  transfers between devices with their start and end apart: 9 -> 15, of which waited for: 9 -> 12; matrix products, arithmetic and copies ran while one was open for 6% -> 10% of each run, Pallas kernels for 0% -> 0%
where the time goes in v1:
time: 1060 us
  waiting for transfers between devices  883 us (83%)
  matrix products  59.5 us (6%)
  local copies, waits for them, and re-layouts  51.5 us (5%)
  other arithmetic  27.4 us (3%)
  between operations  14.8 us (1%)
  blocking collectives  11.6 us (1%)
    ppermute x7, waiting for transfers between devices, on_device(): lax.ppermute(ring[-1], 'req', [(dev, (dev + 1) % 8) for dev in range(8)])  375 us
    all_gather x1, waiting for transfers between devices, on_device(): lax.all_gather(qkv_weight, 'req', axis=0, tiled=True)  170 us
    all_gather x1, waiting for transfers between devices, on_device(): lax.all_gather(gate_up, 'req', axis=1, tiled=True)  146 us
    all_gather x1, waiting for transfers between devices, on_device(): lax.all_gather(down_weight, 'req', axis=1, tiled=True)  113 us
    all_gather x1, waiting for transfers between devices, on_device(): lax.all_gather(out_weight, 'req', axis=1, tiled=True)  52.3 us
    unnamed x63, local copies, waits for them, and re-layouts  44.6 us
  transfers between devices with their start and end apart: 15, of which 12 were waited for; matrix products, arithmetic and copies ran while one was open for 10% of the time, Pallas kernels for 0%

profile of v1, /device:TPU:0, one launch (start us, length us, event | category | flops | bytes accessed | tf_op | source)
XLA Modules:
  0.0 1057.4 jit_solution(7073386201328397894)
XLA Ops:
  11.5 2.8 convert_reduce_fusion
  15.9 3.0 multiply_cosine_fusion.1
  19.0 170.4 %all-gather.5.cloned.1.call-done = bf16[4096,1536]{1,0:T(8,128)(2,1)} async-done(((bf16[512,1536]{1,0:T(8,128)(2,1)}), bf16[4096,1536]{1,0:T(8,128)(2,1)}) %all-gather.5.cloned.1.call-update) | async-done | bytes 12582928 | tf_op jit(solution)/shard_map/all_gather | solution.py:119
  189.4 11.8 %fusion.18 = f32[512,1536]{0,1:T(8,128)S(1)} fusion(bf16[4096,1536]{1,0:T(8,128)(2,1)} %all-gather.5.cloned.1.call-done, bf16[512,4096]{1,0:T(8,128)(2,1)} %param.15, f32[4096]{0:T(1024)S(1)} %bitcast.58, f32[4096]{0:T(1024)S(1)} %bitcast.59, f32[512]{0:T(512)S(1)} %add_rsqrt_fusion.1, f32[512]{0:T(512)S(1)} %broadcast_multiply_fusion.1), kind=kOutput, calls=%fused_computation.27 | convolution fusion | flops 6455033856 | bytes 19959808 | tf_op jit(solution)/shard_map/dot_general | solution.py:117
  209.7 2.7 fusion.46
  212.4 52.3 %all-gather.7.cloned.1.call-done = bf16[512,4096]{1,0:T(8,128)(2,1)} async-done(((bf16[512,512]{1,0:T(8,128)(2,1)}), bf16[512,4096]{1,0:T(8,128)(2,1)}) %all-gather.7.cloned.1.call-update) | async-done | bytes 4194320 | tf_op jit(solution)/shard_map/all_gather | solution.py:131
  264.6 6.6 convolution_convert_fusion.1
  274.2 48.2 %collective-permute-done = bf16[4,1024,256]{2,1,0:T(8,128)(2,1)S(1)} collective-permute-done((bf16[4,1024,256]{2,1,0:T(8,128)(2,1)S(1)}, bf16[4,1024,256]{2,1,0:T(8,128)(2,1)S(1)}, u32[]{:S(2)}, u32[]{:S(2)}) %collective-permute-start) | collective-permute-done | bytes 2097184 | tf_op jit(solution)/shard_map/ppermute | solution.py:171
  323.8 48.9 %collective-permute-done.1 = bf16[4,1024,256]{2,1,0:T(8,128)(2,1)S(1)} collective-permute-done((bf16[4,1024,256]{2,1,0:T(8,128)(2,1)S(1)}, bf16[4,1024,256]{2,1,0:T(8,128)(2,1)S(1)}, u32[]{:S(2)}, u32[]{:S(2)}) %collective-permute-start.1) | collective-permute-done | bytes 2097184 | tf_op jit(solution)/shard_map/ppermute | solution.py:171
  374.0 94.9 %collective-permute-done.2 = bf16[4,1024,256]{2,1,0:T(8,128)(2,1)S(1)} collective-permute-done((bf16[4,1024,256]{2,1,0:T(8,128)(2,1)S(1)}, bf16[4,1024,256]{2,1,0:T(8,128)(2,1)S(1)}, u32[]{:S(2)}, u32[]{:S(2)}) %collective-permute-start.2) | collective-permute-done | bytes 2097184 | tf_op jit(solution)/shard_map/ppermute | solution.py:171
  470.3 85.6 %collective-permute-done.3 = bf16[4,1024,256]{2,1,0:T(8,128)(2,1)} collective-permute-done((bf16[4,1024,256]{2,1,0:T(8,128)(2,1)S(1)}, bf16[4,1024,256]{2,1,0:T(8,128)(2,1)}, u32[]{:S(2)}, u32[]{:S(2)}) %collective-permute-start.3) | collective-permute-done | bytes 2097184 | tf_op jit(solution)/shard_map/ppermute | solution.py:171
  556.1 5.6 convert_reduce_fusion.1
  564.9 146.4 %all-gather.9.cloned.1.call-done = bf16[2,4096,1024]{2,1,0:T(8,128)(2,1)} async-done(((bf16[2,512,1024]{2,1,0:T(8,128)(2,1)}), bf16[2,4096,1024]{2,1,0:T(8,128)(2,1)}) %all-gather.9.cloned.1.call-update) | async-done | bytes 16777232 | tf_op jit(solution)/shard_map/all_gather | solution.py:144
  711.4 15.1 %fusion.36 = f32[2,512,1024]{2,1,0:T(8,128)} fusion(bf16[2,4096,1024]{2,1,0:T(8,128)(2,1)} %all-gather.9.cloned.1.call-done, bf16[512,4096]{1,0:T(8,128)(2,1)} %copy-done.3, f32[4096]{0:T(1024)S(1)} %bitcast.56, f32[4096]{0:T(1024)S(1)} %bitcast.57, f32[512]{0:T(512)S(1)} %add_rsqrt_fusion, f32[512]{0:T(512)S(1)} %broadcast_multiply_fusion), kind=kOutput, calls=%fused_computation.43 | convolution fusion | flops 8602517504 | bytes 25202688 | tf_op jit(solution)/shard_map/rk,pkn->prn/dot_general | solution.py:141
  726.5 113.0 %all-gather.11.cloned.1.call-done = bf16[1024,4096]{1,0:T(8,128)(2,1)} async-done(((bf16[1024,512]{1,0:T(8,128)(2,1)}), bf16[1024,4096]{1,0:T(8,128)(2,1)}) %all-gather.11.cloned.1.call-update) | async-done | bytes 8388624 | tf_op jit(solution)/shard_map/all_gather | solution.py:150
  839.5 11.1 %convolution_convert_fusion = bf16[512,4096]{1,0:T(8,128)(2,1)} fusion(bf16[1024,4096]{1,0:T(8,128)(2,1)} %all-gather.11.cloned.1.call-done, f32[2,512,1024]{2,1,0:T(8,128)} %fusion.36), kind=kOutput, calls=%fused_computation.23 | convolution fusion | flops 4300210176 | bytes 16777216 | tf_op jit(solution)/shard_map/dot_general | solution.py:148
  852.2 48.5 %collective-permute-done.5 = bf16[4,1024,256]{2,1,0:T(8,128)(2,1)} collective-permute-done((bf16[4,1024,256]{2,1,0:T(8,128)(2,1)}, bf16[4,1024,256]{2,1,0:T(8,128)(2,1)}, u32[]{:S(2)}, u32[]{:S(2)}) %collective-permute-start.5) | collective-permute-done | bytes 2097184 | tf_op jit(solution)/shard_map/ppermute | solution.py:171
  901.2 48.7 %collective-permute-done.6 = bf16[4,1024,256]{2,1,0:T(8,128)(2,1)} collective-permute-done((bf16[4,1024,256]{2,1,0:T(8,128)(2,1)}, bf16[4,1024,256]{2,1,0:T(8,128)(2,1)}, u32[]{:S(2)}, u32[]{:S(2)}) %collective-permute-start.6) | collective-permute-done | bytes 2097184 | tf_op jit(solution)/shard_map/ppermute | solution.py:171
  949.9 3.1 constant_dynamic-update-slice_fusion.15
  953.0 3.1 constant_dynamic-update-slice_fusion.14
  956.0 3.2 constant_dynamic-update-slice_fusion.13
  959.3 3.2 constant_dynamic-update-slice_fusion.12
  968.4 3.0 constant_dynamic-update-slice_fusion.7
  971.5 3.1 constant_dynamic-update-slice_fusion.6
  974.5 3.1 constant_dynamic-update-slice_fusion.5
  977.6 3.1 constant_dynamic-update-slice_fusion.4
  992.9 5.7 all-reduce
  998.6 10.1 fusion.33
  1010.6 17.5 %reduce-scatter.5.cloned.1.call-done = bf16[128,512]{1,0:T(8,128)(2,1)} async-done(((bf16[128,2048]{1,0:T(8,128)(2,1)}), bf16[128,512]{1,0:T(8,128)(2,1)}) %reduce-scatter.5.cloned.1.call-update) | async-done | bytes 131088 | tf_op jit(solution)/shard_map/reduce_scatter | solution.py:180
  1030.2 5.5 all-to-all-start
  1036.4 6.7 all-to-all-done
  1043.3 5.9 psum.31
  (131 shorter events, 50.8 us)
Async XLA Ops:
  7.2 1001.6 %copy-start = (s32[1024,1]{0,1:T(1,128)S(1)}, s32[1024,1]{0,1:T(1,128)}, u32[]{:S(2)}) copy-start(s32[1024,1]{0,1:T(1,128)} %param.19) | copy-start | bytes 12292
  7.2 182.2 %all-gather.5.cloned.1.call-start = ((), (), s32[]{:S(2)}) async-start(), calls=%async_computation.3 | async-start | bytes 14155776 | tf_op jit(solution)/shard_map/all_gather | solution.py:119
  7.9 256.7 %all-gather.7.cloned.1.call-start = ((), (), s32[]{:S(2)}) async-start(), calls=%async_computation.4 | async-start | bytes 4718592 | tf_op jit(solution)/shard_map/all_gather | solution.py:131
  8.7 547.4 %all-reduce.3.cloned.1.call-start = ((), (), s32[]{:S(2)}) async-start(), calls=%async_computation.5 | async-start | bytes 8388608 | tf_op jit(solution)/shard_map/psum | solution.py:134
  8.7 5.6 copy-start.2
  11.4 7.5 copy-start.18
  11.4 7.5 copy-start.19
  203.6 2.2 copy-start.11
  203.6 2.2 copy-start.12
  203.6 2.2 copy-start.13
  203.6 2.2 copy-start.14
  271.2 199.1 %copy-start.20 = (f32[2,4096]{1,0:T(2,128)S(1)}, f32[2,4096]{1,0:T(2,128)}, u32[]{:S(2)}) copy-start(f32[2,4096]{1,0:T(2,128)} %param.22) | copy-start | bytes 98308
  271.2 440.2 %all-gather.9.cloned.1.call-start = ((), (), s32[]{:S(2)}) async-start(), calls=%async_computation.6 | async-start | bytes 18874368 | tf_op jit(solution)/shard_map/all_gather | solution.py:144
  271.8 567.7 %all-gather.11.cloned.1.call-start = ((), (), s32[]{:S(2)}) async-start(), calls=%async_computation.7 | async-start | bytes 9437184 | tf_op jit(solution)/shard_map/all_gather | solution.py:150
  272.4 714.3 %reduce-scatter.3.cloned.1.call-start = ((), (), s32[]{:S(2)}) async-start(), calls=%async_computation.8 | async-start | bytes 5242880 | tf_op jit(solution)/shard_map/reduce_scatter | solution.py:153
  272.8 49.6 %collective-permute-start = (bf16[4,1024,256]{2,1,0:T(8,128)(2,1)S(1)}, bf16[4,1024,256]{2,1,0:T(8,128)(2,1)S(1)}, u32[]{:S(2)}, u32[]{:S(2)}) collective-permute-start(bf16[4,1024,256]{2,1,0:T(8,128)(2,1)S(1)} %copy-done.4), channel_id=1, source_target_pairs={{0,4},{4,8},{8,12},{12,16},{16,20},{20,24},{24,28},{28,0},{1,5},{5... | collective-permute-start | bytes 6291464 | tf_op jit(solution)/shard_map/ppermute | solution.py:171
  323.8 48.9 %collective-permute-start.1 = (bf16[4,1024,256]{2,1,0:T(8,128)(2,1)S(1)}, bf16[4,1024,256]{2,1,0:T(8,128)(2,1)S(1)}, u32[]{:S(2)}, u32[]{:S(2)}) collective-permute-start(bf16[4,1024,256]{2,1,0:T(8,128)(2,1)S(1)} %collective-permute-done), channel_id=1, source_target_pairs={{0,4},{4,8},{8,12},{12,16},{16,20},{20,24},{24,28},{28,0},{1,5},{5... | collective-permute-start | bytes 6291464 | tf_op jit(solution)/shard_map/ppermute | solution.py:171
  374.0 94.9 %collective-permute-start.2 = (bf16[4,1024,256]{2,1,0:T(8,128)(2,1)S(1)}, bf16[4,1024,256]{2,1,0:T(8,128)(2,1)S(1)}, u32[]{:S(2)}, u32[]{:S(2)}) collective-permute-start(bf16[4,1024,256]{2,1,0:T(8,128)(2,1)S(1)} %collective-permute-done.1), channel_id=1, source_target_pairs={{0,4},{4,8},{8,12},{12,16},{16,20},{20,24},{24,28},{28,0},{1,5},{5... | collective-permute-start | bytes 6291464 | tf_op jit(solution)/shard_map/ppermute | solution.py:171
  470.3 85.6 %collective-permute-start.3 = (bf16[4,1024,256]{2,1,0:T(8,128)(2,1)S(1)}, bf16[4,1024,256]{2,1,0:T(8,128)(2,1)}, u32[]{:S(2)}, u32[]{:S(2)}) collective-permute-start(bf16[4,1024,256]{2,1,0:T(8,128)(2,1)S(1)} %collective-permute-done.2), channel_id=1, source_target_pairs={{0,4},{4,8},{8,12},{12,16},{16,20},{20,24},{24,28},{28,0},{1,5},{5... | collective-permute-start | bytes 6291464 | tf_op jit(solution)/shard_map/ppermute | solution.py:171
  555.9 294.8 %collective-permute-start.4 = (bf16[4,1024,256]{2,1,0:T(8,128)(2,1)}, bf16[4,1024,256]{2,1,0:T(8,128)(2,1)}, u32[]{:S(2)}, u32[]{:S(2)}) collective-permute-start(bf16[4,1024,256]{2,1,0:T(8,128)(2,1)} %collective-permute-done.3), channel_id=1, source_target_pairs={{0,4},{4,8},{8,12},{12,16},{16,20},{20,24},{24,28},{28,0},{1,5},{5... | collective-permute-start | bytes 6291464 | tf_op jit(solution)/shard_map/ppermute | solution.py:171
  561.6 2.1 copy-start.3
  850.6 50.3 %copy-start.21 = (s32[128,4]{0,1:T(4,128)S(1)}, s32[128,4]{0,1:T(4,128)}, u32[]{:S(2)}) copy-start(s32[128,4]{0,1:T(4,128)} %param.18) | copy-start | bytes 6148
  850.7 177.5 %reduce-scatter.5.cloned.1.call-start = ((), (), s32[]{:S(2)}) async-start(), calls=%async_computation.9 | async-start | bytes 655360 | tf_op jit(solution)/shard_map/reduce_scatter | solution.py:180
  850.7 50.0 %collective-permute-start.5 = (bf16[4,1024,256]{2,1,0:T(8,128)(2,1)}, bf16[4,1024,256]{2,1,0:T(8,128)(2,1)}, u32[]{:S(2)}, u32[]{:S(2)}) collective-permute-start(bf16[4,1024,256]{2,1,0:T(8,128)(2,1)} %collective-permute-done.4), channel_id=1, source_target_pairs={{0,4},{4,8},{8,12},{12,16},{16,20},{20,24},{24,28},{28,0},{1,5},{5... | collective-permute-start | bytes 6291464 | tf_op jit(solution)/shard_map/ppermute | solution.py:171
  900.7 49.2 %collective-permute-start.6 = (bf16[4,1024,256]{2,1,0:T(8,128)(2,1)}, bf16[4,1024,256]{2,1,0:T(8,128)(2,1)}, u32[]{:S(2)}, u32[]{:S(2)}) collective-permute-start(bf16[4,1024,256]{2,1,0:T(8,128)(2,1)} %collective-permute-done.5), channel_id=1, source_target_pairs={{0,4},{4,8},{8,12},{12,16},{16,20},{20,24},{24,28},{28,0},{1,5},{5... | collective-permute-start | bytes 6291464 | tf_op jit(solution)/shard_map/ppermute | solution.py:171
  956.0 6.5 copy-start.10
  959.3 4.7 copy-start.8
  962.5 3.0 copy-start.6
  990.7 7.9 copy-start.16
  990.8 7.9 copy-start.17
  998.6 11.0 %copy-start.1 = (s32[2,2]{1,0:T(2,128)S(1)}, s32[2,2]{1,0:T(2,128)}, u32[]{:S(2)}) copy-start(s32[2,2]{1,0:T(2,128)} %param.16) | copy-start | bytes 52
  1030.2 12.8 %all-to-all-start = ((bf16[8,16,512]{2,1,0:T(8,128)(2,1)}), bf16[8,16,512]{2,1,0:T(8,128)(2,1)S(1)}, u32[]{:S(2)}, u32[]{:S(2)}) async-start(bf16[8,16,512]{2,1,0:T(8,128)(2,1)} %bitcast.18), calls=%async_computation.2 | async-start | bytes 262144 | tf_op jit(solution)/shard_map/all_to_all | solution.py:197
  (5 other events, 7.3 us)
Sparse Core Ops, SparseCore 0:
  10.2 179.1 all-gather.4
  191.4 73.1 all-gather.6
  271.3 83.6 all-reduce.2
  357.3 354.0 all-gather.8
  713.5 125.9 all-gather.10
  850.8 42.6 reduce-scatter.2
  1008.9 19.1 reduce-scatter.4
